TPU v7x, 32 devices: a whole 2x2x4 slice. The times are simulated.
32 devices in a mesh: orb: 8 (over y, x, core), probe: 4 (over z).
Axes of the slice: x: 2, y: 2, z: 4, core: 2. Of those that a mesh axis runs over, the one named last changes fastest.
Arguments:
- tiles: bfloat16 [32, 9, 256, 256], P('orb', None, 'probe'), may hold values from -0.0625 to 0.0625
- pattern: int32 [32, 9], P('orb'), may hold values from 0 to 1, as said below
- signs: int32 [8192, 512], P('orb', 'probe'), may hold values from 0 to 1
- previous: bfloat16 [8192, 512], P('orb', 'probe'), may hold values from -6 to 6
- current: bfloat16 [8192, 512], P('orb', 'probe'), may hold values from -6 to 6
Outputs:
- older: bfloat16 [8192, 512], P('orb', 'probe')
- newest: bfloat16 [8192, 512], P('orb', 'probe')
- moments: float32 [4, 512], P(None, 'probe')
Inputs may be any that keep to these rules, and one draw needn't show every extreme that they name: pattern[I, 4] is 1 for every row block; each row block has 4 to 9 ones; the 4 row blocks of one index of orb hold at most 28 ones together, and some index of orb holds exactly 28.
All inputs are finite; a program needn't handle non-finite values.
Results may differ from a plain program's by a relative error of at most 0.0053.
Values may be sent and summed in bfloat16 or wider, within the bound.
A program may use at most 64 MiB of HBM per device.

v0:
```python
import math
import jax
import jax.numpy as jnp
from jax import lax
from jax.sharding import PartitionSpec as P

REACH = 4
STEPS = 4


def extended(array, sides, width):
    for axis, dim in sides:
        peers, length = (lax.axis_size(axis), array.shape[dim])
        up = [(i, (i + 1) % peers) for i in range(peers)]
        down = [(j, i) for i, j in up]
        last = lax.slice_in_dim(array, length - width, length, axis=dim)
        initial = lax.slice_in_dim(array, 0, width, axis=dim)
        before = lax.ppermute(last, axis, up)
        after = lax.ppermute(initial, axis, down)
        array = jnp.concatenate([before, array, after], axis=dim)
    return array


def extend_panel(vec, block_rows):
    return extended(vec, (("orb", 0),), REACH * block_rows)


def body(tiles, pattern, signs, previous, current):
    row_blocks, offsets, shard_rows, block_rows = tiles.shape
    probe_count = previous.shape[1]
    sign_f = (2 * signs - 1).astype(jnp.float32)
    factor = 1.0 / math.sqrt(lax.axis_size("orb") * row_blocks * block_rows)
    full_tiles = lax.all_gather(tiles, "probe", axis=2, tiled=True)
    mask_b = pattern.astype(jnp.bfloat16)
    older, newest = (previous, current)
    collected = []
    for step in range(STEPS):
        blocks = extend_panel(newest, block_rows).reshape(
            row_blocks + 2 * REACH, block_rows, probe_count
        )
        windows = jnp.stack(
            [blocks[offset : offset + row_blocks] for offset in range(offsets)], axis=1
        )
        windows = windows * mask_b[:, :, None, None]
        total = jnp.einsum(
            "roij,rojp->rip", full_tiles, windows, preferred_element_type=jnp.float32
        )
        image = total.reshape(row_blocks * block_rows, probe_count)
        nxt = (2.0 * image - older.astype(jnp.float32)).astype(jnp.bfloat16)
        local_sum = jnp.sum(sign_f * nxt.astype(jnp.float32), axis=0)
        collected.append(lax.psum(local_sum, "orb") * factor)
        older, newest = (newest, nxt)
    stacked = jnp.stack(collected)
    return (older, newest, stacked)


def solution(mesh):
    placed = (
        P("orb", None, "probe", None),
        P("orb", None),
        P("orb", "probe"),
        P("orb", "probe"),
        P("orb", "probe"),
    )
    return jax.shard_map(
        body,
        mesh=mesh,
        in_specs=placed,
        out_specs=(P("orb", "probe"), P("orb", "probe"), P(None, "probe")),
        check_vma=False,
    )
```

profile of v0, /device:TPU:0, one launch (start us, length us, event | category | flops | bytes accessed | tf_op | source)
XLA Modules:
  0.0 224.4 jit_solution(14347151901448904519)
XLA Ops:
  8.4 2.9 %collective-permute-start.1 = (bf16[1024,128]{1,0:T(8,128)(2,1)}, bf16[1024,128]{1,0:T(8,128)(2,1)S(1)}, u32[]{:S(2)}, u32[]{:S(2)}) collective-permute-start(bf16[1024,128]{1,0:T(8,128)(2,1)} %param.9), channel_id=1, source_target_pairs={{4,0},{8,4},{12,8},{16,12},{20,16},{24,20},{28,24},{0,28},{5,1},{9... | collective-permute-start | bytes 786440 | tf_op jit(solution)/shard_map/ppermute | solution.py:19
  13.2 2.5 %collective-permute-done = bf16[1024,128]{1,0:T(8,128)(2,1)S(1)} collective-permute-done((bf16[1024,128]{1,0:T(8,128)(2,1)}, bf16[1024,128]{1,0:T(8,128)(2,1)S(1)}, u32[]{:S(2)}, u32[]{:S(2)}) %collective-permute-start) | collective-permute-done | bytes 262176 | tf_op jit(solution)/shard_map/ppermute | solution.py:18
  25.3 76.4 %all-gather.2.cloned.1.call-done = bf16[4,9,256,256]{3,2,1,0:T(8,128)(2,1)} async-done(((bf16[4,9,64,256]{3,2,1,0:T(8,128)(2,1)}), bf16[4,9,256,256]{3,2,1,0:T(8,128)(2,1)}) %all-gather.2.cloned.1.call-update) | async-done | bytes 4718608 | tf_op jit(solution)/shard_map/all_gather | solution.py:33
  101.7 4.0 %fusion.41 = f32[4,256,128]{1,2,0:T(8,128)S(1)} fusion(bf16[4,9,256,256]{3,2,1,0:T(8,128)(2,1)} %all-gather.2.cloned.1.call-done, bf16[4,9,256,128]{2,3,1,0:T(8,128)(2,1)S(1)} %constant_dynamic-update-slice_fusion.4, bf16[4,9]{1,0:T(4,128)(2,1)S(1)} %convert_element_type.38), kind=kOutput, calls=%fused_computation.19 | convolution fusion | flops 605290496 | bytes 7602248 | tf_op jit(solution)/shard_map/roij,rojp->rip/dot_general | solution.py:45
  107.0 2.6 %collective-permute-start.3 = (bf16[1024,128]{1,0:T(8,128)(2,1)S(1)}, bf16[1024,128]{1,0:T(8,128)(2,1)S(1)}, u32[]{:S(2)}, u32[]{:S(2)}) collective-permute-start(bf16[1024,128]{1,0:T(8,128)(2,1)S(1)} %fusion.53), channel_id=1, source_target_pairs={{4,0},{8,4},{12,8},{16,12},{20,16},{24,20},{28,24},{0,28},{5,1},{9... | collective-permute-start | bytes 786440 | tf_op jit(solution)/shard_map/ppermute | solution.py:19
  110.5 4.2 %collective-permute-done.2 = bf16[1024,128]{1,0:T(8,128)(2,1)S(1)} collective-permute-done((bf16[1024,128]{1,0:T(8,128)(2,1)S(1)}, bf16[1024,128]{1,0:T(8,128)(2,1)S(1)}, u32[]{:S(2)}, u32[]{:S(2)}) %collective-permute-start.2) | collective-permute-done | bytes 262176 | tf_op jit(solution)/shard_map/ppermute | solution.py:18
  118.4 1.8 copy.56
  120.2 1.8 copy.57
  122.0 1.8 copy.59
  131.7 4.0 %fusion.35 = f32[4,256,128]{1,2,0:T(8,128)S(1)} fusion(bf16[4,9,256,256]{3,2,1,0:T(8,128)(2,1)} %all-gather.2.cloned.1.call-done, bf16[4,9,256,128]{2,3,1,0:T(8,128)(2,1)S(1)} %constant_dynamic-update-slice_fusion.13, bf16[4,9]{1,0:T(4,128)(2,1)S(1)} %convert_element_type.38), kind=kOutput, calls=%fused_computation.17 | convolution fusion | flops 605290496 | bytes 7602248 | tf_op jit(solution)/shard_map/roij,rojp->rip/dot_general | solution.py:45
  139.6 4.7 %collective-permute-done.4 = bf16[1024,128]{1,0:T(8,128)(2,1)S(1)} collective-permute-done((bf16[1024,128]{1,0:T(8,128)(2,1)S(1)}, bf16[1024,128]{1,0:T(8,128)(2,1)S(1)}, u32[]{:S(2)}, u32[]{:S(2)}) %collective-permute-start.4) | collective-permute-done | bytes 262176 | tf_op jit(solution)/shard_map/ppermute | solution.py:18
  148.1 1.8 copy.66
  149.9 1.8 copy.67
  151.7 1.8 copy.69
  161.3 4.8 %fusion.29 = f32[4,256,128]{1,2,0:T(8,128)} fusion(bf16[4,9,256,256]{3,2,1,0:T(8,128)(2,1)} %all-gather.2.cloned.1.call-done, bf16[4,9,256,128]{2,3,1,0:T(8,128)(2,1)S(1)} %constant_dynamic-update-slice_fusion.22, bf16[4,9]{1,0:T(4,128)(2,1)S(1)} %convert_element_type.38), kind=kOutput, calls=%fused_computation.15 | convolution fusion | flops 605290496 | bytes 7602248 | tf_op jit(solution)/shard_map/roij,rojp->rip/dot_general | solution.py:45
  167.5 2.0 collective-permute-start.6
  171.0 5.2 %collective-permute-done.6 = bf16[1024,128]{1,0:T(8,128)(2,1)S(1)} collective-permute-done((bf16[1024,128]{1,0:T(8,128)(2,1)S(1)}, bf16[1024,128]{1,0:T(8,128)(2,1)S(1)}, u32[]{:S(2)}, u32[]{:S(2)}) %collective-permute-start.6) | collective-permute-done | bytes 262176 | tf_op jit(solution)/shard_map/ppermute | solution.py:18
  180.0 1.8 copy.76
  181.8 1.8 copy.77
  183.6 1.8 copy.79
  187.2 1.8 copy.81
  194.9 4.8 %fusion.23 = f32[4,256,128]{1,2,0:T(8,128)} fusion(bf16[4,9,256,256]{3,2,1,0:T(8,128)(2,1)} %all-gather.2.cloned.1.call-done, bf16[4,9,256,128]{2,3,1,0:T(8,128)(2,1)S(1)} %constant_dynamic-update-slice_fusion.31, bf16[4,9]{1,0:T(4,128)(2,1)S(1)} %convert_element_type.38), kind=kOutput, calls=%fused_computation.13 | convolution fusion | flops 605290496 | bytes 7602248 | tf_op jit(solution)/shard_map/roij,rojp->rip/dot_general | solution.py:45
  201.0 2.0 fusion.49
  203.0 13.9 %all-reduce = (f32[128]{0:T(128)S(1)}, f32[128]{0:T(128)S(1)}, f32[128]{0:T(128)S(1)}, f32[128]{0:T(128)S(1)}) all-reduce(f32[128]{0:T(128)S(1)} %get-tuple-element.4, f32[128]{0:T(128)S(1)} %get-tuple-element.5, f32[128]{0:T(128)S(1)} %get-tuple-element.6, f32[128]{0:T(128)S(1)} %get-tuple-element.3), channel_id=1, replica_groups=mesh['orb'=8,'probe'=4] {'orb'}, use_global_device_ids=true, to_apply=%region_7.0 | all-reduce | flops 512 | bytes 4096 | tf_op jit(solution)/shard_map/psum | solution.py:51
  (119 shorter events, 57.7 us)
Async XLA Ops:
  7.2 8.6 %copy-start.1 = (bf16[1024,128]{1,0:T(8,128)(2,1)S(1)}, bf16[1024,128]{1,0:T(8,128)(2,1)}, u32[]{:S(2)}) copy-start(bf16[1024,128]{1,0:T(8,128)(2,1)} %param.9) | copy-start | bytes 786436
  7.2 94.5 %all-gather.2.cloned.1.call-start = ((), (), s32[]{:S(2)}) async-start(), calls=%async_computation | async-start | bytes 5898240 | tf_op jit(solution)/shard_map/all_gather | solution.py:33
  7.9 7.8 %collective-permute-start = (bf16[1024,128]{1,0:T(8,128)(2,1)}, bf16[1024,128]{1,0:T(8,128)(2,1)S(1)}, u32[]{:S(2)}, u32[]{:S(2)}) collective-permute-start(bf16[1024,128]{1,0:T(8,128)(2,1)} %param.9), channel_id=1, source_target_pairs={{0,4},{4,8},{8,12},{12,16},{16,20},{20,24},{24,28},{28,0},{1,5},{5... | collective-permute-start | bytes 786440 | tf_op jit(solution)/shard_map/ppermute | solution.py:18
  8.4 8.9 %collective-permute-start.1 = (bf16[1024,128]{1,0:T(8,128)(2,1)}, bf16[1024,128]{1,0:T(8,128)(2,1)S(1)}, u32[]{:S(2)}, u32[]{:S(2)}) collective-permute-start(bf16[1024,128]{1,0:T(8,128)(2,1)} %param.9), channel_id=1, source_target_pairs={{4,0},{8,4},{12,8},{16,12},{20,16},{24,20},{28,24},{0,28},{5,1},{9... | collective-permute-start | bytes 786440 | tf_op jit(solution)/shard_map/ppermute | solution.py:19
  23.0 2.1 copy-start.5
  23.0 2.2 copy-start.3
  23.0 2.2 copy-start.4
  23.0 2.2 copy-start.2
  107.0 7.7 %collective-permute-start.2 = (bf16[1024,128]{1,0:T(8,128)(2,1)S(1)}, bf16[1024,128]{1,0:T(8,128)(2,1)S(1)}, u32[]{:S(2)}, u32[]{:S(2)}) collective-permute-start(bf16[1024,128]{1,0:T(8,128)(2,1)S(1)} %fusion.53), channel_id=1, source_target_pairs={{0,4},{4,8},{8,12},{12,16},{16,20},{20,24},{24,28},{28,0},{1,5},{5... | collective-permute-start | bytes 786440 | tf_op jit(solution)/shard_map/ppermute | solution.py:18
  107.0 7.7 %collective-permute-start.3 = (bf16[1024,128]{1,0:T(8,128)(2,1)S(1)}, bf16[1024,128]{1,0:T(8,128)(2,1)S(1)}, u32[]{:S(2)}, u32[]{:S(2)}) collective-permute-start(bf16[1024,128]{1,0:T(8,128)(2,1)S(1)} %fusion.53), channel_id=1, source_target_pairs={{4,0},{8,4},{12,8},{16,12},{20,16},{24,20},{28,24},{0,28},{5,1},{9... | collective-permute-start | bytes 786440 | tf_op jit(solution)/shard_map/ppermute | solution.py:19
  126.6 4.9 %copy-start.7 = (bf16[4,1,256,128]{2,3,1,0:T(8,128)(2,1)S(1)}, bf16[4,1,256,128]{2,3,1,0:T(8,128)(2,1)}, u32[]{:S(2)}) copy-start(bf16[4,1,256,128]{2,3,1,0:T(8,128)(2,1)} %copy.60) | copy-start | bytes 786436
  126.6 5.0 %copy-start.8 = (bf16[4,1,256,128]{2,3,1,0:T(8,128)(2,1)S(1)}, bf16[4,1,256,128]{2,3,1,0:T(8,128)(2,1)}, u32[]{:S(2)}) copy-start(bf16[4,1,256,128]{2,3,1,0:T(8,128)(2,1)} %copy.61) | copy-start | bytes 786436
  135.9 8.4 %collective-permute-start.4 = (bf16[1024,128]{1,0:T(8,128)(2,1)S(1)}, bf16[1024,128]{1,0:T(8,128)(2,1)S(1)}, u32[]{:S(2)}, u32[]{:S(2)}) collective-permute-start(bf16[1024,128]{1,0:T(8,128)(2,1)S(1)} %fusion.52), channel_id=1, source_target_pairs={{0,4},{4,8},{8,12},{12,16},{16,20},{20,24},{24,28},{28,0},{1,5},{5... | collective-permute-start | bytes 786440 | tf_op jit(solution)/shard_map/ppermute | solution.py:18
  137.7 6.7 %collective-permute-start.5 = (bf16[1024,128]{1,0:T(8,128)(2,1)S(1)}, bf16[1024,128]{1,0:T(8,128)(2,1)S(1)}, u32[]{:S(2)}, u32[]{:S(2)}) collective-permute-start(bf16[1024,128]{1,0:T(8,128)(2,1)S(1)} %fusion.52), channel_id=1, source_target_pairs={{4,0},{8,4},{12,8},{16,12},{20,16},{24,20},{28,24},{0,28},{5,1},{9... | collective-permute-start | bytes 786440 | tf_op jit(solution)/shard_map/ppermute | solution.py:19
  156.3 4.9 %copy-start.9 = (bf16[4,1,256,128]{2,3,1,0:T(8,128)(2,1)S(1)}, bf16[4,1,256,128]{2,3,1,0:T(8,128)(2,1)}, u32[]{:S(2)}) copy-start(bf16[4,1,256,128]{2,3,1,0:T(8,128)(2,1)} %copy.70) | copy-start | bytes 786436
  156.3 5.0 %copy-start.10 = (bf16[4,1,256,128]{2,3,1,0:T(8,128)(2,1)S(1)}, bf16[4,1,256,128]{2,3,1,0:T(8,128)(2,1)}, u32[]{:S(2)}) copy-start(bf16[4,1,256,128]{2,3,1,0:T(8,128)(2,1)} %copy.71) | copy-start | bytes 786436
  167.4 33.5 %copy-start = (bf16[1024,128]{1,0:T(8,128)(2,1)}, bf16[1024,128]{1,0:T(8,128)(2,1)S(1)}, u32[]{:S(2)}) copy-start(bf16[1024,128]{1,0:T(8,128)(2,1)S(1)} %fusion.48) | copy-start | bytes 786436
  167.5 8.7 %collective-permute-start.6 = (bf16[1024,128]{1,0:T(8,128)(2,1)S(1)}, bf16[1024,128]{1,0:T(8,128)(2,1)S(1)}, u32[]{:S(2)}, u32[]{:S(2)}) collective-permute-start(bf16[1024,128]{1,0:T(8,128)(2,1)S(1)} %fusion.48), channel_id=1, source_target_pairs={{0,4},{4,8},{8,12},{12,16},{16,20},{20,24},{24,28},{28,0},{1,5},{5... | collective-permute-start | bytes 786440 | tf_op jit(solution)/shard_map/ppermute | solution.py:18
  169.5 6.7 %collective-permute-start.7 = (bf16[1024,128]{1,0:T(8,128)(2,1)S(1)}, bf16[1024,128]{1,0:T(8,128)(2,1)S(1)}, u32[]{:S(2)}, u32[]{:S(2)}) collective-permute-start(bf16[1024,128]{1,0:T(8,128)(2,1)S(1)} %fusion.48), channel_id=1, source_target_pairs={{4,0},{8,4},{12,8},{16,12},{20,16},{24,20},{28,24},{0,28},{5,1},{9... | collective-permute-start | bytes 786440 | tf_op jit(solution)/shard_map/ppermute | solution.py:19
  189.9 4.9 %copy-start.11 = (bf16[4,1,256,128]{2,3,1,0:T(8,128)(2,1)S(1)}, bf16[4,1,256,128]{2,3,1,0:T(8,128)(2,1)}, u32[]{:S(2)}) copy-start(bf16[4,1,256,128]{2,3,1,0:T(8,128)(2,1)} %copy.80) | copy-start | bytes 786436
  189.9 5.0 %copy-start.12 = (bf16[4,1,256,128]{2,3,1,0:T(8,128)(2,1)S(1)}, bf16[4,1,256,128]{2,3,1,0:T(8,128)(2,1)}, u32[]{:S(2)}) copy-start(bf16[4,1,256,128]{2,3,1,0:T(8,128)(2,1)} %copy.81) | copy-start | bytes 786436
  189.9 5.0 %copy-start.6 = (bf16[4,1,256,128]{2,3,1,0:T(8,128)(2,1)S(1)}, bf16[4,1,256,128]{2,3,1,0:T(8,128)(2,1)}, u32[]{:S(2)}) copy-start(bf16[4,1,256,128]{2,3,1,0:T(8,128)(2,1)} %copy.82) | copy-start | bytes 786436
Sparse Core Ops, SparseCore 0:
  9.6 92.0 all-gather.1
where the time goes:
time: 226 us; the launch traced here: 224 us
  waiting for transfers between devices  95.2 us (42%)
  local copies, waits for them, and re-layouts  63.6 us (28%)
  matrix products  17.6 us (8%)
  between operations  14.6 us (6%)
  blocking collectives  13.9 us (6%)
  starting transfers between devices  11.7 us (5%)
  other arithmetic  7.73 us (3%)
    all_gather x1, waiting for transfers between devices, body(): full_tiles = lax.all_gather(tiles, 'probe', axis=2, tiled=True)  76.4 us
    another operation x40, local copies, waits for them, and re-layouts, body(): jnp.stack([blocks[offset:offset + row_blocks] for offset in range(offsets...  40.6 us
    unnamed x60, local copies, waits for them, and re-layouts  20 us
    dot_general x4, matrix products, body(): jnp.einsum('roij,rojp->rip', full_tiles, windows, preferred_element_type=...  17.6 us
    ppermute x4, waiting for transfers between devices, extended(): before = lax.ppermute(last, axis, up)  16.6 us
    psum x1, blocking collectives, body(): collected.append(lax.psum(local_sum, 'orb') * factor)  13.9 us
    ppermute x4, starting transfers between devices, extended(): after = lax.ppermute(initial, axis, down)  7.37 us
  transfers between devices with their start and end apart: 9, of which 6 were waited for; matrix products, arithmetic and copies ran while one was open for 5% of the time, Pallas kernels for 0%

commit v1 on v0

--- a/solution.py
+++ b/solution.py
@@ -30,7 +30,32 @@
     probe_count = previous.shape[1]
     sign_f = (2 * signs - 1).astype(jnp.float32)
     factor = 1.0 / math.sqrt(lax.axis_size("orb") * row_blocks * block_rows)
-    full_tiles = lax.all_gather(tiles, "probe", axis=2, tiled=True)
+    local_part, kept_arr, a_next = (
+        jax.lax.axis_size("probe"),
+        jax.lax.axis_index("probe"),
+        tiles.shape[2],
+    )
+    copies = [ii * local_part if w == 2 else ii for w, ii in enumerate(tiles.shape)]
+    full_tiles = lax.dynamic_update_slice_in_dim(
+        jnp.zeros(copies, tiles.dtype), tiles, kept_arr * a_next, axis=2
+    )
+    later = row_out = tiles
+    p = 1
+    while p < local_part // 2 + 1:
+        later = jax.lax.ppermute(
+            later, "probe", [(w, (w + 1) % local_part) for w in range(local_part)]
+        )
+        full_tiles = lax.dynamic_update_slice_in_dim(
+            full_tiles, later, (kept_arr - p) % local_part * a_next, axis=2
+        )
+        if 2 * p < local_part:
+            row_out = jax.lax.ppermute(
+                row_out, "probe", [(w, (w - 1) % local_part) for w in range(local_part)]
+            )
+            full_tiles = lax.dynamic_update_slice_in_dim(
+                full_tiles, row_out, (kept_arr + p) % local_part * a_next, axis=2
+            )
+        p += 1
     mask_b = pattern.astype(jnp.bfloat16)
     older, newest = (previous, current)
     collected = []

time: 226 us -> 131 us (0.58)
  local copies, waits for them, and re-layouts: 63.6 us -> 3.78 us
  between operations: 14.6 us -> 1.12 us
  matrix products: 17.6 us -> 5.8 us
  waiting for transfers between devices: 95.2 us -> 87.7 us
  other arithmetic: 7.73 us -> 2.95 us
  starting transfers between devices: 11.7 us -> 15.8 us
    all_gather x1 -> x0, waiting for transfers between devices: 76.4 us -> none  [body(): full_tiles = lax.all_gather(tiles, 'probe', axis=2, tiled=True)]
    ppermute x0 -> x3, waiting for transfers between devices: none -> 69.3 us  [the longest x2 44.7 us: body(): jax.lax.ppermute(later, 'probe', [(w, (w + 1) % local_part) for w in rang...]
    another operation x40 -> x4, local copies, waits for them, and re-layouts: 40.6 us -> 0.15 us  [body(): jnp.stack([blocks[offset:offset + row_blocks] for offset in range(offsets...]
    unnamed x60 -> x44, local copies, waits for them, and re-layouts: 20 us -> 2.34 us
    dot_general x4, matrix products: 17.6 us -> 5.8 us  [body(): jnp.einsum('roij,rojp->rip', full_tiles, windows, preferred_element_type=...]
    ppermute x0 -> x3, starting transfers between devices: none -> 5.24 us  [the longest x2 3.08 us: body(): jax.lax.ppermute(later, 'probe', [(w, (w + 1) % local_part) for w in rang...]
    mul x4 -> x0, local copies, waits for them, and re-layouts: 2.84 us -> none  [body(): nxt = (2.0 * image - older.astype(jnp.float32)).astype(jnp.bfloat16)]
    concatenate x3, other arithmetic: 3.25 us -> 0.52 us  [extended(): array = jnp.concatenate([before, array, after], axis=dim)]
  transfers between devices with their start and end apart: 9 -> 11, of which waited for: 6 -> 8; matrix products, arithmetic and copies ran while one was open for 5% -> 2% of each run, Pallas kernels for 0% -> 0%
where the time goes in v1:
time: 131 us
  waiting for transfers between devices  87.7 us (67%)
  starting transfers between devices  15.8 us (12%)
  blocking collectives  13.5 us (10%)
  matrix products  5.8 us (4%)
  local copies, waits for them, and re-layouts  3.78 us (3%)
  other arithmetic  2.95 us (2%)
    ppermute x2, waiting for transfers between devices, body(): jax.lax.ppermute(later, 'probe', [(w, (w + 1) % local_part) for w in rang...  44.7 us
    ppermute x1, waiting for transfers between devices, body(): jax.lax.ppermute(row_out, 'probe', [(w, (w - 1) % local_part) for w in ra...  24.6 us
    ppermute x4, waiting for transfers between devices, extended(): before = lax.ppermute(last, axis, up)  17.2 us
    psum x1, blocking collectives, body(): collected.append(lax.psum(local_sum, 'orb') * factor)  13.5 us
    ppermute x4, starting transfers between devices, extended(): after = lax.ppermute(initial, axis, down)  6.81 us
    dot_general x4, matrix products, body(): jnp.einsum('roij,rojp->rip', full_tiles, windows, preferred_element_type=...  5.8 us
    ppermute x4, starting transfers between devices, extended(): before = lax.ppermute(last, axis, up)  3.78 us
    ppermute x2, starting transfers between devices, body(): jax.lax.ppermute(later, 'probe', [(w, (w + 1) % local_part) for w in rang...  3.08 us
  transfers between devices with their start and end apart: 11, of which 8 were waited for; matrix products, arithmetic and copies ran while one was open for 2% of the time, Pallas kernels for 0%

profile of v1, /device:TPU:0, one launch (start us, length us, event | category | flops | bytes accessed | tf_op | source)
XLA Modules:
  0.0 130.7 jit_solution(7487607436983973827)
XLA Ops:
  0.6 3.1 %collective-permute-start = (bf16[4,9,64,256]{3,2,1,0:T(8,128)(2,1)}, bf16[4,9,64,256]{3,2,1,0:T(8,128)(2,1)S(1)}, u32[]{:S(2)}, u32[]{:S(2)}) collective-permute-start(bf16[4,9,64,256]{3,2,1,0:T(8,128)(2,1)} %param.5), channel_id=1, source_target_pairs={{0,1},{1,2},{2,3},{3,0},{4,5},{5,6},{6,7},{7,4},{8,9},{9,10},{10,1... | collective-permute-start | bytes 3538952 | tf_op jit(solution)/shard_map/ppermute | solution.py:45
  3.7 2.2 %collective-permute-start.1 = (bf16[4,9,64,256]{3,2,1,0:T(8,128)(2,1)}, bf16[4,9,64,256]{3,2,1,0:T(8,128)(2,1)S(1)}, u32[]{:S(2)}, u32[]{:S(2)}) collective-permute-start(bf16[4,9,64,256]{3,2,1,0:T(8,128)(2,1)} %param.5), channel_id=1, source_target_pairs={{0,3},{1,0},{2,1},{3,2},{4,7},{5,4},{6,5},{7,6},{8,11},{9,8},{10,9... | collective-permute-start | bytes 3538952 | tf_op jit(solution)/shard_map/ppermute | solution.py:52
  5.9 2.3 %collective-permute-start.4 = (bf16[1024,128]{1,0:T(8,128)(2,1)}, bf16[1024,128]{1,0:T(8,128)(2,1)S(1)}, u32[]{:S(2)}, u32[]{:S(2)}) collective-permute-start(bf16[1024,128]{1,0:T(8,128)(2,1)} %param.9), channel_id=1, source_target_pairs={{4,0},{8,4},{12,8},{16,12},{20,16},{24,20},{28,24},{0,28},{5,1},{9... | collective-permute-start | bytes 786440 | tf_op jit(solution)/shard_map/ppermute | solution.py:19
  8.2 0.7 convert_element_type.38
  9.4 0.7 copy-done.2
  11.1 1.2 collective-permute-done.4
  12.6 20.2 %collective-permute-done = bf16[4,9,64,256]{3,2,1,0:T(8,128)(2,1)S(1)} collective-permute-done((bf16[4,9,64,256]{3,2,1,0:T(8,128)(2,1)}, bf16[4,9,64,256]{3,2,1,0:T(8,128)(2,1)S(1)}, u32[]{:S(2)}, u32[]{:S(2)}) %collective-permute-start) | collective-permute-done | bytes 1179680 | tf_op jit(solution)/shard_map/ppermute | solution.py:45
  33.3 24.6 %collective-permute-done.1 = bf16[4,9,64,256]{3,2,1,0:T(8,128)(2,1)S(1)} collective-permute-done((bf16[4,9,64,256]{3,2,1,0:T(8,128)(2,1)}, bf16[4,9,64,256]{3,2,1,0:T(8,128)(2,1)S(1)}, u32[]{:S(2)}, u32[]{:S(2)}) %collective-permute-start.1) | collective-permute-done | bytes 1179680 | tf_op jit(solution)/shard_map/ppermute | solution.py:52
  58.0 24.5 %collective-permute-done.2 = bf16[4,9,64,256]{3,2,1,0:T(8,128)(2,1)S(1)} collective-permute-done((bf16[4,9,64,256]{3,2,1,0:T(8,128)(2,1)S(1)}, bf16[4,9,64,256]{3,2,1,0:T(8,128)(2,1)S(1)}, u32[]{:S(2)}, u32[]{:S(2)}) %collective-permute-start.2) | collective-permute-done | bytes 1179680 | tf_op jit(solution)/shard_map/ppermute | solution.py:45
  82.7 1.4 %fusion.29 = f32[4,256,128]{2,1,0:T(8,128)S(1)} fusion(bf16[4,9,256,256]{3,2,1,0:T(8,128)(2,1)S(1)} %constant_dynamic-update-slice_fusion.40, bf16[4,9,256,128]{3,2,1,0:T(8,128)(2,1)S(1)} %constant_dynamic-update-slice_fusion.4, bf16[4,9]{1,0:T(4,128)(2,1)S(1)} %convert_element_type.38), kind=kOutput, calls=%fused_computation.15 | convolution fusion | flops 605290496 | bytes 7602248 | tf_op jit(solution)/shard_map/roij,rojp->rip/dot_general | solution.py:70
  84.3 2.6 %collective-permute-start.6 = (bf16[1024,128]{1,0:T(8,128)(2,1)S(1)}, bf16[1024,128]{1,0:T(8,128)(2,1)S(1)}, u32[]{:S(2)}, u32[]{:S(2)}) collective-permute-start(bf16[1024,128]{1,0:T(8,128)(2,1)S(1)} %fusion.41), channel_id=1, source_target_pairs={{4,0},{8,4},{12,8},{16,12},{20,16},{24,20},{28,24},{0,28},{5,1},{9... | collective-permute-start | bytes 786440 | tf_op jit(solution)/shard_map/ppermute | solution.py:19
  86.9 5.0 %collective-permute-done.5 = bf16[1024,128]{1,0:T(8,128)(2,1)S(1)} collective-permute-done((bf16[1024,128]{1,0:T(8,128)(2,1)S(1)}, bf16[1024,128]{1,0:T(8,128)(2,1)S(1)}, u32[]{:S(2)}, u32[]{:S(2)}) %collective-permute-start.5) | collective-permute-done | bytes 262176 | tf_op jit(solution)/shard_map/ppermute | solution.py:18
  92.4 1.4 %fusion.26 = f32[4,256,128]{2,1,0:T(8,128)S(1)} fusion(bf16[4,9,256,256]{3,2,1,0:T(8,128)(2,1)S(1)} %constant_dynamic-update-slice_fusion.40, bf16[4,9,256,128]{3,2,1,0:T(8,128)(2,1)S(1)} %constant_dynamic-update-slice_fusion.13, bf16[4,9]{1,0:T(4,128)(2,1)S(1)} %convert_element_type.38), kind=kOutput, calls=%fused_computation.14 | convolution fusion | flops 605290496 | bytes 7602248 | tf_op jit(solution)/shard_map/roij,rojp->rip/dot_general | solution.py:70
  94.0 1.8 %collective-permute-start.7 = (bf16[1024,128]{1,0:T(8,128)(2,1)S(1)}, bf16[1024,128]{1,0:T(8,128)(2,1)S(1)}, u32[]{:S(2)}, u32[]{:S(2)}) collective-permute-start(bf16[1024,128]{1,0:T(8,128)(2,1)S(1)} %fusion.40), channel_id=1, source_target_pairs={{0,4},{4,8},{8,12},{12,16},{16,20},{20,24},{24,28},{28,0},{1,5},{5... | collective-permute-start | bytes 786440 | tf_op jit(solution)/shard_map/ppermute | solution.py:18
  95.8 1.1 collective-permute-start.8
  96.9 5.6 %collective-permute-done.7 = bf16[1024,128]{1,0:T(8,128)(2,1)S(1)} collective-permute-done((bf16[1024,128]{1,0:T(8,128)(2,1)S(1)}, bf16[1024,128]{1,0:T(8,128)(2,1)S(1)}, u32[]{:S(2)}, u32[]{:S(2)}) %collective-permute-start.7) | collective-permute-done | bytes 262176 | tf_op jit(solution)/shard_map/ppermute | solution.py:18
  103.0 1.4 %fusion.23 = f32[4,256,128]{2,1,0:T(8,128)S(1)} fusion(bf16[4,9,256,256]{3,2,1,0:T(8,128)(2,1)S(1)} %constant_dynamic-update-slice_fusion.40, bf16[4,9,256,128]{3,2,1,0:T(8,128)(2,1)S(1)} %constant_dynamic-update-slice_fusion.22, bf16[4,9]{1,0:T(4,128)(2,1)S(1)} %convert_element_type.38), kind=kOutput, calls=%fused_computation.13 | convolution fusion | flops 605290496 | bytes 7602248 | tf_op jit(solution)/shard_map/roij,rojp->rip/dot_general | solution.py:70
  104.6 1.9 %collective-permute-start.9 = (bf16[1024,128]{1,0:T(8,128)(2,1)S(1)}, bf16[1024,128]{1,0:T(8,128)(2,1)S(1)}, u32[]{:S(2)}, u32[]{:S(2)}) collective-permute-start(bf16[1024,128]{1,0:T(8,128)(2,1)S(1)} %fusion.36), channel_id=1, source_target_pairs={{0,4},{4,8},{8,12},{12,16},{16,20},{20,24},{24,28},{28,0},{1,5},{5... | collective-permute-start | bytes 786440 | tf_op jit(solution)/shard_map/ppermute | solution.py:18
  106.5 0.8 collective-permute-start.10
  107.3 6.3 %collective-permute-done.9 = bf16[1024,128]{1,0:T(8,128)(2,1)S(1)} collective-permute-done((bf16[1024,128]{1,0:T(8,128)(2,1)S(1)}, bf16[1024,128]{1,0:T(8,128)(2,1)S(1)}, u32[]{:S(2)}, u32[]{:S(2)}) %collective-permute-start.9) | collective-permute-done | bytes 262176 | tf_op jit(solution)/shard_map/ppermute | solution.py:18
  114.1 1.4 %fusion.20 = f32[4,256,128]{2,1,0:T(8,128)S(1)} fusion(bf16[4,9,256,256]{3,2,1,0:T(8,128)(2,1)S(1)} %constant_dynamic-update-slice_fusion.40, bf16[4,9,256,128]{3,2,1,0:T(8,128)(2,1)S(1)} %constant_dynamic-update-slice_fusion.31, bf16[4,9]{1,0:T(4,128)(2,1)S(1)} %convert_element_type.38), kind=kOutput, calls=%fused_computation.12 | convolution fusion | flops 605290496 | bytes 7602248 | tf_op jit(solution)/shard_map/roij,rojp->rip/dot_general | solution.py:70
  115.6 1.0 fusion.37
  116.6 13.5 %all-reduce = (f32[128]{0:T(128)S(1)}, f32[128]{0:T(128)S(1)}, f32[128]{0:T(128)S(1)}, f32[128]{0:T(128)S(1)}) all-reduce(f32[128]{0:T(128)S(1)} %get-tuple-element.4, f32[128]{0:T(128)S(1)} %get-tuple-element.5, f32[128]{0:T(128)S(1)} %get-tuple-element.6, f32[128]{0:T(128)S(1)} %get-tuple-element.3), channel_id=1, replica_groups=mesh['orb'=8,'probe'=4] {'orb'}, use_global_device_ids=true, to_apply=%region_7.8 | all-reduce | flops 512 | bytes 4096 | tf_op jit(solution)/shard_map/psum | solution.py:76
  130.1 0.6 pad_maximum_fusion.6
  (71 shorter events, 4.2 us)
Async XLA Ops:
  0.6 32.2 %collective-permute-start = (bf16[4,9,64,256]{3,2,1,0:T(8,128)(2,1)}, bf16[4,9,64,256]{3,2,1,0:T(8,128)(2,1)S(1)}, u32[]{:S(2)}, u32[]{:S(2)}) collective-permute-start(bf16[4,9,64,256]{3,2,1,0:T(8,128)(2,1)} %param.5), channel_id=1, source_target_pairs={{0,1},{1,2},{2,3},{3,0},{4,5},{5,6},{6,7},{7,4},{8,9},{9,10},{10,1... | collective-permute-start | bytes 3538952 | tf_op jit(solution)/shard_map/ppermute | solution.py:45
  3.7 6.9 %collective-permute-start.3 = (bf16[1024,128]{1,0:T(8,128)(2,1)}, bf16[1024,128]{1,0:T(8,128)(2,1)S(1)}, u32[]{:S(2)}, u32[]{:S(2)}) collective-permute-start(bf16[1024,128]{1,0:T(8,128)(2,1)} %param.9), channel_id=1, source_target_pairs={{0,4},{4,8},{8,12},{12,16},{16,20},{20,24},{24,28},{28,0},{1,5},{5... | collective-permute-start | bytes 786440 | tf_op jit(solution)/shard_map/ppermute | solution.py:18
  3.7 54.1 %collective-permute-start.1 = (bf16[4,9,64,256]{3,2,1,0:T(8,128)(2,1)}, bf16[4,9,64,256]{3,2,1,0:T(8,128)(2,1)S(1)}, u32[]{:S(2)}, u32[]{:S(2)}) collective-permute-start(bf16[4,9,64,256]{3,2,1,0:T(8,128)(2,1)} %param.5), channel_id=1, source_target_pairs={{0,3},{1,0},{2,1},{3,2},{4,7},{5,4},{6,5},{7,6},{8,11},{9,8},{10,9... | collective-permute-start | bytes 3538952 | tf_op jit(solution)/shard_map/ppermute | solution.py:52
  5.9 6.5 %collective-permute-start.4 = (bf16[1024,128]{1,0:T(8,128)(2,1)}, bf16[1024,128]{1,0:T(8,128)(2,1)S(1)}, u32[]{:S(2)}, u32[]{:S(2)}) collective-permute-start(bf16[1024,128]{1,0:T(8,128)(2,1)} %param.9), channel_id=1, source_target_pairs={{4,0},{8,4},{12,8},{16,12},{20,16},{24,20},{28,24},{0,28},{5,1},{9... | collective-permute-start | bytes 786440 | tf_op jit(solution)/shard_map/ppermute | solution.py:19
  8.9 1.3 copy-start.2
  10.1 0.9 copy-start.1
  32.8 49.7 %collective-permute-start.2 = (bf16[4,9,64,256]{3,2,1,0:T(8,128)(2,1)S(1)}, bf16[4,9,64,256]{3,2,1,0:T(8,128)(2,1)S(1)}, u32[]{:S(2)}, u32[]{:S(2)}) collective-permute-start(bf16[4,9,64,256]{3,2,1,0:T(8,128)(2,1)S(1)} %collective-permute-done), channel_id=1, source_target_pairs={{0,1},{1,2},{2,3},{3,0},{4,5},{5,6},{6,7},{7,4},{8,9},{9,10},{10,1... | collective-permute-start | bytes 3538952 | tf_op jit(solution)/shard_map/ppermute | solution.py:45
  82.7 1.5 %copy-start.4 = (bf16[1024,128]{1,0:T(8,128)(2,1)S(1)}, bf16[1024,128]{1,0:T(8,128)(2,1)}, u32[]{:S(2)}) copy-start(bf16[1024,128]{1,0:T(8,128)(2,1)} %param.8) | copy-start | bytes 786436
  84.2 7.6 %collective-permute-start.5 = (bf16[1024,128]{1,0:T(8,128)(2,1)S(1)}, bf16[1024,128]{1,0:T(8,128)(2,1)S(1)}, u32[]{:S(2)}, u32[]{:S(2)}) collective-permute-start(bf16[1024,128]{1,0:T(8,128)(2,1)S(1)} %fusion.41), channel_id=1, source_target_pairs={{0,4},{4,8},{8,12},{12,16},{16,20},{20,24},{24,28},{28,0},{1,5},{5... | collective-permute-start | bytes 786440 | tf_op jit(solution)/shard_map/ppermute | solution.py:18
  84.3 7.6 %collective-permute-start.6 = (bf16[1024,128]{1,0:T(8,128)(2,1)S(1)}, bf16[1024,128]{1,0:T(8,128)(2,1)S(1)}, u32[]{:S(2)}, u32[]{:S(2)}) collective-permute-start(bf16[1024,128]{1,0:T(8,128)(2,1)S(1)} %fusion.41), channel_id=1, source_target_pairs={{4,0},{8,4},{12,8},{16,12},{20,16},{24,20},{28,24},{0,28},{5,1},{9... | collective-permute-start | bytes 786440 | tf_op jit(solution)/shard_map/ppermute | solution.py:19
  94.0 8.5 %collective-permute-start.7 = (bf16[1024,128]{1,0:T(8,128)(2,1)S(1)}, bf16[1024,128]{1,0:T(8,128)(2,1)S(1)}, u32[]{:S(2)}, u32[]{:S(2)}) collective-permute-start(bf16[1024,128]{1,0:T(8,128)(2,1)S(1)} %fusion.40), channel_id=1, source_target_pairs={{0,4},{4,8},{8,12},{12,16},{16,20},{20,24},{24,28},{28,0},{1,5},{5... | collective-permute-start | bytes 786440 | tf_op jit(solution)/shard_map/ppermute | solution.py:18
  95.8 6.7 %collective-permute-start.8 = (bf16[1024,128]{1,0:T(8,128)(2,1)S(1)}, bf16[1024,128]{1,0:T(8,128)(2,1)S(1)}, u32[]{:S(2)}, u32[]{:S(2)}) collective-permute-start(bf16[1024,128]{1,0:T(8,128)(2,1)S(1)} %fusion.40), channel_id=1, source_target_pairs={{4,0},{8,4},{12,8},{16,12},{20,16},{24,20},{28,24},{0,28},{5,1},{9... | collective-permute-start | bytes 786440 | tf_op jit(solution)/shard_map/ppermute | solution.py:19
  104.5 11.0 %copy-start = (bf16[1024,128]{1,0:T(8,128)(2,1)}, bf16[1024,128]{1,0:T(8,128)(2,1)S(1)}, u32[]{:S(2)}) copy-start(bf16[1024,128]{1,0:T(8,128)(2,1)S(1)} %fusion.36) | copy-start | bytes 786436
  104.6 9.0 %collective-permute-start.9 = (bf16[1024,128]{1,0:T(8,128)(2,1)S(1)}, bf16[1024,128]{1,0:T(8,128)(2,1)S(1)}, u32[]{:S(2)}, u32[]{:S(2)}) collective-permute-start(bf16[1024,128]{1,0:T(8,128)(2,1)S(1)} %fusion.36), channel_id=1, source_target_pairs={{0,4},{4,8},{8,12},{12,16},{16,20},{20,24},{24,28},{28,0},{1,5},{5... | collective-permute-start | bytes 786440 | tf_op jit(solution)/shard_map/ppermute | solution.py:18
  106.5 7.1 %collective-permute-start.10 = (bf16[1024,128]{1,0:T(8,128)(2,1)S(1)}, bf16[1024,128]{1,0:T(8,128)(2,1)S(1)}, u32[]{:S(2)}, u32[]{:S(2)}) collective-permute-start(bf16[1024,128]{1,0:T(8,128)(2,1)S(1)} %fusion.36), channel_id=1, source_target_pairs={{4,0},{8,4},{12,8},{16,12},{20,16},{24,20},{28,24},{0,28},{5,1},{9... | collective-permute-start | bytes 786440 | tf_op jit(solution)/shard_map/ppermute | solution.py:19
  114.1 1.5 %copy-start.3 = (s32[1024,128]{1,0:T(8,128)S(1)}, s32[1024,128]{1,0:T(8,128)}, u32[]{:S(2)}) copy-start(s32[1024,128]{1,0:T(8,128)} %param.7) | copy-start | bytes 1572868
